TPU v7x, 128 devices: a whole 4x4x4 slice. The times are simulated.
128 devices in a mesh: pb: 16 (over z, x_lo, core), tile: 8 (over x_hi, y).
Axes of the slice: x: 4 (x_hi: 2, x_lo: 2; x = x_hi * 2 + x_lo), y: 4, z: 4, core: 2. Of those that a mesh axis runs over, the one named last changes fastest.
Arguments:
- trials: bfloat16 [16, 4, 4096], P('pb', None, 'tile'), may hold values from -6 to 6
- w_screen: bfloat16 [16, 2048, 2048], P('pb', 'tile'), may hold values from -48 to 48
- cond_bands: bfloat16 [16, 2048, 64], P('pb', 'tile'), may hold values from -0.125 to 0.125
- val_bands: bfloat16 [16, 2048, 64], P('pb', 'tile'), may hold values from -0.125 to 0.125
- pair_table: int32 [16, 16], replicated, may hold values from 0 to 15, as said below
Outputs:
- applied: bfloat16 [16, 4, 4096], P('pb', None, 'tile')
Inputs may be any that keep to these rules, and one draw needn't show every extreme that they name: Every row and every column of pair_table holds each k-point exactly once.
All inputs are finite; a program needn't handle non-finite values.
Results may differ from a plain program's by a relative error of at most 0.023.
Values may be sent and summed in bfloat16 or wider, within the bound.
A program may use at most 128 MiB of HBM per device.

v0:
```python
import jax
import jax.numpy as jnp
from jax import lax
from jax.experimental import pallas as pl
from jax.experimental.pallas import tpu as pltpu
from jax.sharding import PartitionSpec as P

MESH = pl.DeviceIdType.MESH
bf16 = jnp.bfloat16
f32 = jnp.float32
NN = (((1,), (0,)), ((), ()))
NT = (((1,), (1,)), ((), ()))
TN = (((0,), (0,)), ((), ()))

OWN_X, OWN_UP, OWN_DN, OWN_SIB = 0, 1, 2, 3
XC_UP, XC_DN, XC_SIB = 4, 5, 6
FAR_UP, FAR_DN = (7, 8), (9, 10)
DN_SIB, UP_SIB, FAR_SIB = (11, 12), (13, 14), (15, 16)
KINDS = 17


def dot(a, b, dims):
    return lax.dot_general(a, b, dims, preferred_element_type=f32)


def kernel(
    x_ref, w_ref, ucin_ref, uvin_ref, tab_ref, out_ref,
    uv, xb, uc, p0, p1, a0, a1, g, yout, yin, y2out, y2in, xs, os,
    tsend, trecv, ucsend, ucrecv, isend, irecv, ysend, yrecv, zsend, zrecv,
):
    q = lax.axis_index("pb")
    t = lax.axis_index("tile")
    z, h, c = q // 4, (q // 2) % 2, q % 2

    def kof(dz, dh, dc):
        return ((z + dz) % 4) * 4 + ((h + dh) % 2) * 2 + (c + dc) % 2

    me = kof(0, 0, 0)

    barrier = pltpu.get_barrier_semaphore()
    for j in range(1, 16):
        pl.semaphore_signal(barrier, inc=1, device_id=((q + j) % 16, t), device_id_type=MESH)
    for j in range(1, 8):
        pl.semaphore_signal(barrier, inc=1, device_id=(q, (t + j) % 8), device_id_type=MESH)

    uv[me, t] = jnp.transpose(uvin_ref[0].astype(f32)).astype(bf16)
    uc[z, q % 4] = jnp.transpose(ucin_ref[0].astype(f32)).astype(bf16)
    xin = x_ref[0].astype(f32)
    for s in range(4):
        for b in range(8):
            xs[(s // 2) * 8 + b : (s // 2) * 8 + b + 1, (s % 2) * 64 : (s % 2) * 64 + 64] = xin[
                s : s + 1, b * 64 : b * 64 + 64
            ]
    xb[me, t] = xs[...].astype(bf16)

    pl.semaphore_wait(barrier, 22)

    def remote(src, dst, ssem, rsem, pb, tile):
        return pltpu.make_async_remote_copy(
            src_ref=src, dst_ref=dst, send_sem=ssem, recv_sem=rsem,
            device_id=(pb, tile), device_id_type=MESH,
        )

    def tcopy(j, owner, peer):
        return (
            remote(uv.at[me, owner], uv.at[me, owner], tsend.at[0, j], trecv.at[0, j], q, peer),
            remote(xb.at[me, owner], xb.at[me, owner], tsend.at[1, j], trecv.at[1, j], q, peer),
        )

    def ccopy(j, owner_z, peer):
        blk = uc.at[owner_z, q % 4]
        return remote(blk, blk, ucsend.at[j], ucrecv.at[j], peer, t)

    def ccolumn(j, dh, dc, peer):
        blk = uc.at[:, kof(0, dh, dc) % 4]
        return remote(blk, blk, ucsend.at[j], ucrecv.at[j], peer, t)

    sib, xnb, up, dn = kof(0, 0, 1), kof(0, 1, 0), kof(1, 0, 0), kof(3, 0, 0)

    for j in range(1, 8):
        for copy in tcopy(j, t, (t + j) % 8):
            copy.start()
    for j in range(1, 4):
        ccopy(j, z, kof(j, 0, 0)).start()
    for j in range(1, 4):
        ccopy(j, (z - j + 4) % 4, q).wait_recv()
    ccolumn(4, 0, 0, xnb).start()
    ccolumn(5, 0, 0, sib).start()

    def record(kind, k, peer, part=None):
        at = (k,) if part is None else (k, pl.ds(part * 4, 4))
        return (
            remote(uv.at[at], uv.at[at], isend.at[0, kind], irecv.at[0, kind], peer, t),
            remote(xb.at[at], xb.at[at], isend.at[1, kind], irecv.at[1, kind], peer, t),
        )

    def send(*args):
        for copy in record(*args):
            copy.start()

    def take(*args):
        for copy in record(*args):
            copy.wait_recv()

    def boundary_0():
        for j in range(1, 8):
            for copy in tcopy(j, (t - j + 8) % 8, t):
                copy.wait_recv()
        send(OWN_SIB, me, sib)
        send(OWN_X, me, xnb)
        send(OWN_UP, me, up)
        send(OWN_DN, me, dn)

    def boundary_1():
        take(OWN_SIB, kof(0, 0, 1), q)

    def boundary_2():
        k = kof(0, 1, 0)
        take(OWN_X, k, q)
        send(XC_SIB, k, sib)
        send(XC_UP, k, up)
        send(XC_DN, k, dn)

    def pass_on(dh, from_dn, from_up):
        k = kof(3, dh, 0)
        take(from_dn, k, q)
        send(DN_SIB[dh], k, sib)
        send(FAR_UP[dh], k, up, 0)
        k = kof(1, dh, 0)
        take(from_up, k, q)
        send(UP_SIB[dh], k, sib)
        send(FAR_DN[dh], k, dn, 1)

    def boundary_3():
        take(XC_SIB, kof(0, 1, 1), q)
        pass_on(0, OWN_UP, OWN_DN)

    def boundary_5():
        take(DN_SIB[0], kof(3, 0, 1), q)

    def boundary_6():
        pass_on(1, XC_UP, XC_DN)

    def far(dh):
        k = kof(2, dh, 0)
        take(FAR_UP[dh], k, q, 0)
        take(FAR_DN[dh], k, q, 1)
        send(FAR_SIB[dh], k, sib)

    def boundary_7():
        take(UP_SIB[0], kof(1, 0, 1), q)

    def boundary_8():
        far(0)

    def boundary_9():
        take(DN_SIB[1], kof(3, 1, 1), q)

    def boundary_10():
        far(1)

    def boundary_11():
        take(UP_SIB[1], kof(1, 1, 1), q)

    def boundary_13():
        take(FAR_SIB[0], kof(2, 0, 1), q)

    def boundary_15():
        take(FAR_SIB[1], kof(2, 1, 1), q)

    def item(b2, dc):
        dz = jnp.where(b2 < 2, 0, jnp.where(b2 >= 6, 2, jnp.where(b2 % 2 == 0, 3, 1)))
        dh = jnp.where(b2 < 2, b2, jnp.where(b2 < 4, 0, jnp.where(b2 < 6, 1, b2 - 6)))
        return kof(dz, dh, dc)

    def amat(k, a):
        u = uc[k // 4, k % 4]
        xk = xb[k].astype(f32)
        for sh in range(2):
            xm = xk[:, sh * 8 : sh * 8 + 8, :].reshape(64, 128).astype(bf16)
            both = dot(u, xm, TN).astype(bf16)
            a[2 * sh] = both[:, :64]
            a[2 * sh + 1] = both[:, 64:]

    def pmat(k, a, p, b):
        n = slice(b * 256, b * 256 + 256)
        wb = w_ref[0, :, n].astype(f32)
        for s in range(4):
            p[s, :, n] = (dot(a[s], uv[k, b], NN) * wb).astype(bf16)

    def partner(kp):
        k = jnp.int32(0)
        for i in range(1, 16):
            k = jnp.where(tab_ref[i, q] == kp, i, k)
        return k

    def gmat(u, kp, p, b):
        n = slice(b * 256, b * 256 + 256)
        for s in range(4):
            g[kp, s * 64 : s * 64 + 64, n] = dot(u, p[s, :, n], NN).astype(bf16)

    def half(b2, dc, b2n, dcn, pr, pw, an):
        kp, kn = item(b2, dc), item(b2n, dcn)
        kk = partner(kp)
        u = uc[kk // 4, kk % 4]
        amat(kn, an)
        for b in range(8):
            gmat(u, kp, pr, b)
            pmat(kn, an, pw, b)

    boundary_0()
    amat(me, a0)
    for b in range(8):
        pmat(me, a0, p0, b)
    ccolumn(4, 1, 0, q).wait_recv()
    ccolumn(6, 1, 0, sib).start()
    ccolumn(5, 0, 1, q).wait_recv()
    ccolumn(6, 1, 1, q).wait_recv()

    odd = {1: boundary_1, 3: boundary_3, 5: boundary_5, 7: boundary_7, 9: boundary_9, 11: boundary_11, 13: boundary_13}
    even = {2: boundary_2, 6: boundary_6, 8: boundary_8, 10: boundary_10}

    def body(j, carry):
        for b, act in odd.items():
            pl.when(2 * j + 1 == b)(act)
        half(j, 0, j, 1, p0, p1, a1)
        for b, act in even.items():
            pl.when(2 * j + 2 == b)(act)
        half(j, 1, j + 1, 0, p1, p0, a0)
        return carry

    lax.fori_loop(0, 7, body, 0)
    boundary_15()
    half(7, 0, 7, 1, p0, p1, a1)
    last = item(7, 1)
    kk = partner(last)
    u = uc[kk // 4, kk % 4]
    for b in range(8):
        gmat(u, last, p1, b)

    def ycopy(j, owner, k, peer):
        return remote(yout.at[k], yin.at[owner], ysend.at[j], yrecv.at[j], peer, t)

    def ymat(k):
        kp = tab_ref[k, q]
        acc = jnp.zeros((256, 64), f32)
        for b in range(8):
            acc = acc + dot(g[kp, :, b * 256 : b * 256 + 256], uv[k, b], NT)
        both = jnp.concatenate([acc[:128], acc[128:]], axis=1)
        return jnp.swapaxes(both.reshape(2, 8, 8, 128), 0, 1).reshape(8, 16, 128)

    def ybody(j, carry):
        k = (q + j) % 16
        yout[k] = ymat(k).astype(bf16)
        ycopy(j, q, k, k).start()
        return carry

    lax.fori_loop(1, 16, ybody, 0)
    total = ymat(q)
    for j in range(1, 16):
        owner = (q - j + 16) % 16
        ycopy(j, owner, q, q).wait_recv()
        total = total + yin[owner].astype(f32)
    y2out[...] = total.astype(bf16)

    def zcopy(j, owner, part, peer):
        return remote(y2out.at[part], y2in.at[owner], zsend.at[j], zrecv.at[j], q, peer)

    for j in range(1, 8):
        zcopy(j, t, (t + j) % 8, (t + j) % 8).start()
    res = y2out[t].astype(f32)
    for j in range(1, 8):
        owner = (t - j + 8) % 8
        zcopy(j, owner, t, t).wait_recv()
        res = res + y2in[owner].astype(f32)
    for s in range(4):
        for b in range(8):
            os[s : s + 1, b * 64 : b * 64 + 64] = res[
                (s % 2) * 8 + b : (s % 2) * 8 + b + 1, (s // 2) * 64 : (s // 2) * 64 + 64
            ]
    out_ref[0] = os[...].astype(bf16)

    for j in range(1, 8):
        for copy in tcopy(j, t, (t + j) % 8):
            copy.wait_send()
        zcopy(j, t, (t + j) % 8, (t + j) % 8).wait_send()
    for j in range(1, 4):
        ccopy(j, z, kof(j, 0, 0)).wait_send()
    ccolumn(4, 0, 0, xnb).wait_send()
    ccolumn(5, 0, 0, sib).wait_send()
    ccolumn(6, 1, 0, sib).wait_send()
    halves = {FAR_UP[0]: 0, FAR_UP[1]: 0, FAR_DN[0]: 1, FAR_DN[1]: 1}
    for kind in range(KINDS):
        for copy in record(kind, me, sib, halves.get(kind)):
            copy.wait_send()
    for j in range(1, 16):
        ycopy(j, q, (q + j) % 16, (q + j) % 16).wait_send()


def shards(trials, w_screen, cond_bands, val_bands, pair_table):
    vmem = pl.BlockSpec(memory_space=pltpu.VMEM)
    smem = pl.BlockSpec(memory_space=pltpu.SMEM)
    dma = pltpu.SemaphoreType.DMA
    return pl.pallas_call(
        kernel,
        out_shape=jax.ShapeDtypeStruct(trials.shape, bf16),
        in_specs=[vmem, vmem, vmem, vmem, smem],
        out_specs=vmem,
        scratch_shapes=[
            pltpu.VMEM((16, 8, 64, 256), bf16),
            pltpu.VMEM((16, 8, 16, 128), bf16),
            pltpu.VMEM((4, 4, 64, 256), bf16),
            pltpu.VMEM((4, 256, 2048), bf16),
            pltpu.VMEM((4, 256, 2048), bf16),
            pltpu.VMEM((4, 256, 64), bf16),
            pltpu.VMEM((4, 256, 64), bf16),
            pltpu.VMEM((16, 256, 2048), bf16),
            pltpu.VMEM((16, 8, 16, 128), bf16),
            pltpu.VMEM((16, 8, 16, 128), bf16),
            pltpu.VMEM((8, 16, 128), bf16),
            pltpu.VMEM((8, 16, 128), bf16),
            pltpu.VMEM((16, 128), f32),
            pltpu.VMEM((4, 512), f32),
            dma((2, 8)), dma((2, 8)),
            dma((8,)), dma((8,)),
            dma((2, KINDS)), dma((2, KINDS)),
            dma((16,)), dma((16,)),
            dma((8,)), dma((8,)),
        ],
        compiler_params=pltpu.CompilerParams(
            collective_id=0, has_side_effects=True, vmem_limit_bytes=50 * 2**20
        ),
    )(trials, w_screen, cond_bands, val_bands, pair_table)


def solution(mesh):
    in_specs = (
        P("pb", None, "tile"),
        P("pb", "tile", None),
        P("pb", "tile", None),
        P("pb", "tile", None),
        P(),
    )
    out_specs = P("pb", None, "tile")
    return jax.shard_map(shards, mesh=mesh, in_specs=in_specs, out_specs=out_specs, check_vma=False)
```

profile of v0, /device:TPU:1, one launch (start us, length us, event | category | flops | bytes accessed | tf_op | source)
XLA Modules:
  0.0 73.7 jit_solution(2951061249227257731)
XLA Ops:
  0.0 0.0 copy-start.3
  0.0 0.9 %copy.6.ucin_ref = bf16[1,256,64]{2,1,0:T(8,128)(2,1)S(1)} copy(bf16[1,256,64]{1,2,0:T(8,128)(2,1)} %param.7) | data formatting | bytes 65536 | tf_op args[2]
  0.9 0.0 copy-done.3
  0.9 0.0 copy-start.1
  0.9 0.0 copy-start.2
  0.9 0.1 copy.7.uvin_ref
  1.0 0.6 copy-done.1
  1.6 0.0 copy-done.2
  1.6 0.0 copy-start
  1.6 1.2 %copy-done = bf16[1,256,2048]{2,1,0:T(8,128)(2,1)S(1)} copy-done((bf16[1,256,2048]{2,1,0:T(8,128)(2,1)S(1)}, bf16[1,256,2048]{2,1,0:T(8,128)(2,1)}, u32[]{:S(2)}) %copy-start) | copy-done | bytes 1048600
  2.8 70.2 %shard_map.55 = bf16[1,4,512]{2,1,0:T(4,128)(2,1)S(1)} custom-call(bf16[1,4,512]{2,1,0:T(4,128)(2,1)S(1)} %copy-done.2, bf16[1,256,2048]{2,1,0:T(8,128)(2,1)S(1)} %copy-done, bf16[1,256,64]{2,1,0:T(8,128)(2,1)S(1)} %copy.6.ucin_ref, bf16[1,256,64]{2,1,0:T(8,128)(2,1)S(1)} %copy.7.uvin_ref, s32[16,16]{1,0:T(8,128)S(1)} %copy-done.1), custom_call_target="tpu_custom_call" | custom-call | tf_op jit(solution)/shard_map/pallas_call | solution.py:304
  73.1 0.6 copy.9
Async XLA Ops:
  0.0 0.9 %copy-start.3 = (bf16[1,256,64]{1,2,0:T(8,128)(2,1)S(1)}, bf16[1,256,64]{1,2,0:T(8,128)(2,1)}, u32[]{:S(2)}) copy-start(bf16[1,256,64]{1,2,0:T(8,128)(2,1)} %param.8) | copy-start | bytes 98308
  0.9 0.7 copy-start.1
  0.9 0.7 copy-start.2
  1.6 1.2 %copy-start = (bf16[1,256,2048]{2,1,0:T(8,128)(2,1)S(1)}, bf16[1,256,2048]{2,1,0:T(8,128)(2,1)}, u32[]{:S(2)}) copy-start(bf16[1,256,2048]{2,1,0:T(8,128)(2,1)} %w_ref.1) | copy-start | bytes 3145732
where the time goes:
time: 73.9 us; the launch traced here: 73.7 us
  Pallas kernels  70.2 us (95%)
  local copies, waits for them, and re-layouts  3.39 us (5%)
    pallas_call x1, Pallas kernels, shards(): pl.pallas_call(kernel, out_shape=jax.ShapeDtypeStruct(trials.shape, bf16)...  70.2 us
    unnamed x11, local copies, waits for them, and re-layouts  3.39 us

commit v1 on v0

v1 whole, which is shorter than its diff:
```python
import jax
import jax.numpy as jnp
from jax import lax
from jax.experimental import pallas as pl
from jax.experimental.pallas import tpu as pltpu
from jax.sharding import PartitionSpec as P

MESH = pl.DeviceIdType.MESH
bf16 = jnp.bfloat16
f32 = jnp.float32
NN = (((1,), (0,)), ((), ()))
NT = (((1,), (1,)), ((), ()))
TN = (((0,), (0,)), ((), ()))

OWN_X, OWN_UP, OWN_DN, OWN_SIB = (0, 1), (2, 3), (4, 5), (6, 7)
XC_UP, XC_DN, XC_SIB = (8, 9), (10, 11), (12, 13)
FAR_UP, FAR_DN = (14, 15), (16, 17)
DN_SIB, UP_SIB, FAR_SIB = (18, 19), (20, 21), (22, 23)
KINDS = 24
VMEM_LIMIT = 64 * 2**20 - 2**16
WHOLE = (18, 19, 20, 21, 22, 23)


def dot(a, b, dims):
    return lax.dot_general(a, b, dims, preferred_element_type=f32)


def kernel(
    x_hbm, w_hbm, uc_hbm, uv_hbm, tab_hbm, out_ref,
    x_ref, w_ref, tab_ref, uv, xb, uc, p0, p1, a0, a1, g, ysout, ysin, yout, yin, xs, os,
    lsem, tsend, trecv, ucsend, ucrecv, isend, irecv, ssend, srecv, ysend, yrecv,
):
    q = lax.axis_index("pb")
    t = lax.axis_index("tile")
    z, h, c = q // 4, (q // 2) % 2, q % 2
    hi, y = t // 4, t % 4

    def kof(dz, dh, dc):
        return ((z + dz) % 4) * 4 + ((h + dh) % 2) * 2 + (c + dc) % 2

    me = kof(0, 0, 0)
    local = (
        pltpu.make_async_copy(x_hbm.at[0], x_ref, lsem.at[0]),
        pltpu.make_async_copy(uv_hbm.at[0], uv.at[me, t], lsem.at[1]),
        pltpu.make_async_copy(uc_hbm.at[0], uc.at[z, q % 4], lsem.at[2]),
        pltpu.make_async_copy(w_hbm.at[0], w_ref, lsem.at[3]),
        pltpu.make_async_copy(tab_hbm, tab_ref, lsem.at[4]),
    )
    for copy in local:
        copy.start()

    barrier = pltpu.get_barrier_semaphore()
    for j in range(1, 8):
        pl.semaphore_signal(barrier, inc=1, device_id=(q, (t + j) % 8), device_id_type=MESH)
    for j in range(1, 16):
        pl.semaphore_signal(barrier, inc=1, device_id=((q + j) % 16, t), device_id_type=MESH)

    local[0].wait()
    xin = x_ref[...].astype(f32)
    for s in range(4):
        for b in range(8):
            xs[(s // 2) * 8 + b : (s // 2) * 8 + b + 1, (s % 2) * 64 : (s % 2) * 64 + 64] = xin[
                s : s + 1, b * 64 : b * 64 + 64
            ]
    xb[me, t] = xs[...].astype(bf16)
    local[1].wait()
    local[2].wait()

    pl.semaphore_wait(barrier, 22)

    def remote(src, dst, ssem, rsem, pb, tile):
        return pltpu.make_async_remote_copy(
            src_ref=src, dst_ref=dst, send_sem=ssem, recv_sem=rsem,
            device_id=(pb, tile), device_id_type=MESH,
        )

    def at_offset(j, sign):
        return ((hi + j // 4) % 2) * 4 + (y + sign * (j % 4) + 4) % 4

    def tcopy(j, owner, peer):
        return (
            remote(xb.at[me, owner], xb.at[me, owner], tsend.at[1, j], trecv.at[1, j], q, peer),
            remote(uv.at[me, owner], uv.at[me, owner], tsend.at[0, j], trecv.at[0, j], q, peer),
        )

    def ccopy(kind, dz, dh, dc, peer):
        blk = uc.at[(z + dz) % 4, kof(0, dh, dc) % 4]
        return remote(blk, blk, ucsend.at[kind], ucrecv.at[kind], peer, t)

    sib, xnb, up, dn = kof(0, 0, 1), kof(0, 1, 0), kof(1, 0, 0), kof(3, 0, 0)

    def spread(dz):
        ccopy(4 + dz, dz, 0, 0, xnb).start()
        ccopy(8 + dz, dz, 0, 0, sib).start()

    def record(kind, k, peer, first=None):
        at = (k,) if first is None else (k, pl.ds(first * 4, 4))
        return (
            remote(xb.at[at], xb.at[at], isend.at[1, kind], irecv.at[1, kind], peer, t),
            remote(uv.at[at], uv.at[at], isend.at[0, kind], irecv.at[0, kind], peer, t),
        )

    def send(*args):
        for copy in record(*args):
            copy.start()

    def take(*args):
        for copy in record(*args):
            copy.wait_recv()

    def part(i):
        return (hi + i) % 2

    def send_own(i):
        send(OWN_X[i], me, xnb, part(i))
        send(OWN_UP[i], me, up, part(i))
        send(OWN_DN[i], me, dn, part(i))
        send(OWN_SIB[i], me, sib, part(i))

    def x_item(i):
        k = kof(0, 1, 0)
        take(OWN_X[i], k, q, part(i))
        send(XC_UP[i], k, up, part(i))
        send(XC_DN[i], k, dn, part(i))
        send(XC_SIB[i], k, sib, part(i))

    def pass_on(dh, from_dn, from_up):
        k = kof(3, dh, 0)
        for i in range(2):
            take(from_dn[i], k, q, part(i))
        send(FAR_UP[dh], k, up, 0)
        send(DN_SIB[dh], k, sib)
        k = kof(1, dh, 0)
        for i in range(2):
            take(from_up[i], k, q, part(i))
        send(FAR_DN[dh], k, dn, 1)
        send(UP_SIB[dh], k, sib)

    def boundary_3():
        for i in range(2):
            take(XC_SIB[i], kof(0, 1, 1), q, part(i))

    def boundary_5():
        take(DN_SIB[0], kof(3, 0, 1), q)

    def boundary_6():
        pass_on(1, XC_UP, XC_DN)

    def far(dh):
        k = kof(2, dh, 0)
        take(FAR_UP[dh], k, q, 0)
        take(FAR_DN[dh], k, q, 1)
        send(FAR_SIB[dh], k, sib)

    def boundary_7():
        take(UP_SIB[0], kof(1, 0, 1), q)

    def boundary_8():
        far(0)

    def boundary_9():
        take(DN_SIB[1], kof(3, 1, 1), q)

    def boundary_10():
        far(1)

    def boundary_11():
        take(UP_SIB[1], kof(1, 1, 1), q)

    def boundary_13():
        take(FAR_SIB[0], kof(2, 0, 1), q)

    def boundary_15():
        take(FAR_SIB[1], kof(2, 1, 1), q)

    def item(b2, dc):
        dz = jnp.where(b2 < 2, 0, jnp.where(b2 >= 6, 2, jnp.where(b2 % 2 == 0, 3, 1)))
        dh = jnp.where(b2 < 2, b2, jnp.where(b2 < 4, 0, jnp.where(b2 < 6, 1, b2 - 6)))
        return kof(dz, dh, dc)

    def amat(k, a):
        u = uc[k // 4, k % 4]
        xk = xb[k].astype(f32)
        for sh in range(2):
            xm = xk[:, sh * 8 : sh * 8 + 8, :].reshape(64, 128).astype(bf16)
            both = dot(u, xm, TN).astype(bf16)
            a[2 * sh] = both[:, :64]
            a[2 * sh + 1] = both[:, 64:]

    def pmat(k, a, p, b):
        n = slice(b * 256, b * 256 + 256)
        wb = w_ref[:, n].astype(f32)
        for s in range(4):
            p[s, :, n] = (dot(a[s], uv[k, b], NN) * wb).astype(bf16)

    def partner(kp):
        k = jnp.int32(0)
        for i in range(1, 16):
            k = jnp.where(tab_ref[i, q] == kp, i, k)
        return k

    def gmat(u, kp, p, b):
        n = slice(b * 256, b * 256 + 256)
        for s in range(4):
            g[kp, s * 64 : s * 64 + 64, n] = dot(u, p[s, :, n], NN).astype(bf16)

    def half(b2, dc, b2n, dcn, pr, pw, an):
        kp, kn = item(b2, dc), item(b2n, dcn)
        kk = partner(kp)
        u = uc[kk // 4, kk % 4]
        amat(kn, an)
        for b in range(8):
            gmat(u, kp, pr, b)
            pmat(kn, an, pw, b)

    def gmat_all(b2, dc, p):
        kp = item(b2, dc)
        kk = partner(kp)
        u = uc[kk // 4, kk % 4]
        for b in range(8):
            gmat(u, kp, p, b)

    def pmat_all(b2, dc, a, p):
        k = item(b2, dc)
        amat(k, a)
        for b in range(8):
            pmat(k, a, p, b)

    for j in range(1, 4):
        ccopy(j, 0, 0, 0, kof(j, 0, 0)).start()
    for j in (6, 5, 7, 4, 2, 1, 3):
        for copy in tcopy(j, t, at_offset(j, 1)):
            copy.start()
    spread(0)
    for j in (1, 3):
        ccopy(j, 4 - j, 0, 0, q).wait_recv()
        spread(4 - j)
    for j in range(1, 4):
        for copy in tcopy(j, at_offset(j, -1), t):
            copy.wait_recv()
    send_own(0)
    ccopy(2, 2, 0, 0, q).wait_recv()
    spread(2)
    for j in range(4, 8):
        for copy in tcopy(j, at_offset(j, -1), t):
            copy.wait_recv()
    send_own(1)
    for j in (0, 1, 3, 2):
        ccopy(4 + j, j, 1, 0, q).wait_recv()
        ccopy(12 + j, j, 1, 0, sib).start()
    local[3].wait()
    local[4].wait()
    pmat_all(0, 0, a0, p0)
    x_item(0)
    for i in range(2):
        take(OWN_SIB[i], kof(0, 0, 1), q, part(i))
    for j in range(4):
        ccopy(8 + j, j, 0, 1, q).wait_recv()
        ccopy(12 + j, j, 1, 1, q).wait_recv()
    pmat_all(0, 1, a1, p1)
    gmat_all(0, 0, p0)
    x_item(1)
    gmat_all(0, 1, p1)
    pass_on(0, OWN_UP, OWN_DN)
    pmat_all(1, 0, a0, p0)

    odd = {3: boundary_3, 5: boundary_5, 7: boundary_7, 9: boundary_9, 11: boundary_11, 13: boundary_13}
    even = {6: boundary_6, 8: boundary_8, 10: boundary_10}

    def body(j, carry):
        for b, act in odd.items():
            pl.when(2 * j + 3 == b)(act)
        half(j + 1, 0, j + 1, 1, p0, p1, a1)
        for b, act in even.items():
            pl.when(2 * j + 4 == b)(act)
        half(j + 1, 1, j + 2, 0, p1, p0, a0)
        return carry

    lax.fori_loop(0, 6, body, 0)
    boundary_15()
    half(7, 0, 7, 1, p0, p1, a1)
    gmat_all(7, 1, p1)

    def ymat(k):
        kp = tab_ref[k, q]
        acc = jnp.zeros((256, 64), f32)
        for b in range(8):
            acc = acc + dot(g[kp, :, b * 256 : b * 256 + 256], uv[k, b], NT)
        both = jnp.concatenate([acc[:128], acc[128:]], axis=1)
        return jnp.swapaxes(both.reshape(2, 8, 8, 128), 0, 1).reshape(8, 16, 128)

    chip = q // 2

    def scopy(m):
        return remote(ysout.at[m], ysin.at[m], ssend.at[m], srecv.at[m], sib, t)

    def to_sibling(j, carry):
        m = (chip + j) % 8
        ysout[m] = ymat(m * 2 + 1 - c).astype(bf16)
        scopy(m).start()
        return carry

    lax.fori_loop(1, 9, to_sibling, 0)

    def ycopy(j, m, owner, peer):
        return remote(yout.at[m, peer], yin.at[chip, owner], ysend.at[j], yrecv.at[j], m * 2 + c, peer)

    own = pltpu.make_async_copy(yout.at[chip, t], yin.at[chip, t], yrecv.at[0])

    def to_owners(j, carry):
        m = (chip + j) % 8
        part_sum = ymat(m * 2 + c)
        scopy(m).wait_recv()
        yout[m] = (part_sum + ysin[m].astype(f32)).astype(bf16)
        for i in range(8):
            ycopy(j, m, t, (t + i) % 8).start()
        return carry

    lax.fori_loop(1, 8, to_owners, 0)
    part_sum = ymat(q)
    scopy(chip).wait_recv()
    yout[chip] = (part_sum + ysin[chip].astype(f32)).astype(bf16)
    for i in range(1, 8):
        ycopy(0, chip, t, (t + i) % 8).start()
    own.start()

    res = jnp.zeros((16, 128), f32)
    for j in (1, 2, 3, 4, 5, 6, 7, 0):
        m = (chip - j + 8) % 8
        pltpu.make_async_copy(yin.at[m], yin.at[m], yrecv.at[j]).wait()
        res = res + jnp.sum(yin[m].astype(f32), axis=0)
    for s in range(4):
        for b in range(8):
            os[s : s + 1, b * 64 : b * 64 + 64] = res[
                (s % 2) * 8 + b : (s % 2) * 8 + b + 1, (s // 2) * 64 : (s // 2) * 64 + 64
            ]
    out_ref[0] = os[...].astype(bf16)

    for j in range(1, 8):
        for copy in tcopy(j, t, at_offset(j, 1)):
            copy.wait_send()
        pltpu.make_async_copy(yout.at[j], yout.at[j], ysend.at[j]).wait()
    pltpu.make_async_copy(yout.at[0, pl.ds(0, 7)], yout.at[0, pl.ds(0, 7)], ysend.at[0]).wait()
    for j in range(8):
        scopy(j).wait_send()
    for j in range(1, 16):
        ccopy(j, 0, 0, 0, sib).wait_send()
    for kind in range(KINDS):
        for copy in record(kind, me, sib, None if kind in WHOLE else 0):
            copy.wait_send()


def shards(trials, w_screen, cond_bands, val_bands, pair_table):
    vmem = pl.BlockSpec(memory_space=pltpu.VMEM)
    hbm = pl.BlockSpec(memory_space=pltpu.HBM)
    dma = pltpu.SemaphoreType.DMA
    return pl.pallas_call(
        kernel,
        out_shape=jax.ShapeDtypeStruct(trials.shape, bf16),
        in_specs=[hbm] * 5,
        out_specs=vmem,
        scratch_shapes=[
            pltpu.VMEM((4, 512), bf16),
            pltpu.VMEM((256, 2048), bf16),
            pltpu.SMEM((16, 16), jnp.int32),
            pltpu.VMEM((16, 8, 64, 256), bf16),
            pltpu.VMEM((16, 8, 16, 128), bf16),
            pltpu.VMEM((4, 4, 64, 256), bf16),
            pltpu.VMEM((4, 256, 2048), bf16),
            pltpu.VMEM((4, 256, 2048), bf16),
            pltpu.VMEM((4, 256, 64), bf16),
            pltpu.VMEM((4, 256, 64), bf16),
            pltpu.VMEM((16, 256, 2048), bf16),
            pltpu.VMEM((8, 8, 16, 128), bf16),
            pltpu.VMEM((8, 8, 16, 128), bf16),
            pltpu.VMEM((8, 8, 16, 128), bf16),
            pltpu.VMEM((8, 8, 16, 128), bf16),
            pltpu.VMEM((16, 128), f32),
            pltpu.VMEM((4, 512), f32),
            dma((5,)),
            dma((2, 8)), dma((2, 8)),
            dma((16,)), dma((16,)),
            dma((2, KINDS)), dma((2, KINDS)),
            dma((8,)), dma((8,)),
            dma((8,)), dma((8,)),
        ],
        compiler_params=pltpu.CompilerParams(
            collective_id=0, has_side_effects=True, vmem_limit_bytes=VMEM_LIMIT
        ),
    )(trials, w_screen, jnp.swapaxes(cond_bands, 1, 2), jnp.swapaxes(val_bands, 1, 2), pair_table)


def solution(mesh):
    in_specs = (
        P("pb", None, "tile"),
        P("pb", "tile", None),
        P("pb", "tile", None),
        P("pb", "tile", None),
        P(),
    )
    out_specs = P("pb", None, "tile")
    return jax.shard_map(shards, mesh=mesh, in_specs=in_specs, out_specs=out_specs, check_vma=False)
```

time: 73.9 us -> 68.9 us (0.932)
  Pallas kernels: 70.2 us -> 67.5 us
  local copies, waits for them, and re-layouts: 3.39 us -> 1.28 us
    pallas_call x1, Pallas kernels: 70.2 us -> 67.5 us  [shards(): pl.pallas_call(kernel, out_shape=jax.ShapeDtypeStruct(trials.shape, bf16)...]
    unnamed x11 -> x1, local copies, waits for them, and re-layouts: 3.39 us -> 1.28 us
where the time goes in v1:
time: 68.9 us; the launch traced here: 68.7 us
  Pallas kernels  67.5 us (98%)
  local copies, waits for them, and re-layouts  1.28 us (2%)
    pallas_call x1, Pallas kernels, shards(): pl.pallas_call(kernel, out_shape=jax.ShapeDtypeStruct(trials.shape, bf16)...  67.5 us

profile of v1, /device:TPU:1, one launch (start us, length us, event | category | flops | bytes accessed | tf_op | source)
XLA Modules:
  0.0 68.7 jit_solution(15569273469345918776)
XLA Ops:
  0.0 67.5 %shard_map.55 = bf16[1,4,512]{2,1,0:T(4,128)(2,1)} custom-call(bf16[1,4,512]{2,1,0:T(4,128)(2,1)} %x_hbm.1, bf16[1,256,2048]{2,1,0:T(8,128)(2,1)} %w_hbm.1, bf16[1,64,256]{2,1,0:T(8,128)(2,1)} %bitcast.2, bf16[1,64,256]{2,1,0:T(8,128)(2,1)} %bitcast.3, s32[16,16]{1,0:T(8,128)} %tab_hbm.1), custom_call_target="tpu_custom_call" | custom-call | tf_op jit(solution)/shard_map/pallas_call | solution.py:357
  67.5 1.3 %copy.7 = bf16[1,4,512]{2,1,0:T(4,128)(2,1)} copy(bf16[1,4,512]{2,1,0:T(4,128)(2,1)} %shard_map.55) | data formatting | bytes 8192

commit v2 on v1

--- a/solution.py
+++ b/solution.py
@@ -17,7 +17,7 @@
 FAR_UP, FAR_DN = (14, 15), (16, 17)
 DN_SIB, UP_SIB, FAR_SIB = (18, 19), (20, 21), (22, 23)
 KINDS = 24
-VMEM_LIMIT = 64 * 2**20 - 2**16
+VMEM_LIMIT = 60 * 2**20
 WHOLE = (18, 19, 20, 21, 22, 23)
 
 
@@ -89,9 +89,7 @@
 
     sib, xnb, up, dn = kof(0, 0, 1), kof(0, 1, 0), kof(1, 0, 0), kof(3, 0, 0)
 
-    def spread(dz):
-        ccopy(4 + dz, dz, 0, 0, xnb).start()
-        ccopy(8 + dz, dz, 0, 0, sib).start()
+    away = ((2, 1), (2, 0), (1, 1), (3, 1), (1, 0), (3, 0), (0, 1))
 
     def record(kind, k, peer, first=None):
         at = (k,) if first is None else (k, pl.ds(first * 4, 4))
@@ -226,38 +224,33 @@
         for b in range(8):
             pmat(k, a, p, b)
 
-    for j in range(1, 4):
-        ccopy(j, 0, 0, 0, kof(j, 0, 0)).start()
     for j in (6, 5, 7, 4, 2, 1, 3):
         for copy in tcopy(j, t, at_offset(j, 1)):
             copy.start()
-    spread(0)
-    for j in (1, 3):
-        ccopy(j, 4 - j, 0, 0, q).wait_recv()
-        spread(4 - j)
+    for dz, dh in away:
+        ccopy(dz * 2 + dh, 0, 0, 0, kof(dz, dh, 0)).start()
+    ccopy(8, 0, 0, 0, sib).start()
     for j in range(1, 4):
         for copy in tcopy(j, at_offset(j, -1), t):
             copy.wait_recv()
     send_own(0)
-    ccopy(2, 2, 0, 0, q).wait_recv()
-    spread(2)
     for j in range(4, 8):
         for copy in tcopy(j, at_offset(j, -1), t):
             copy.wait_recv()
     send_own(1)
-    for j in (0, 1, 3, 2):
-        ccopy(4 + j, j, 1, 0, q).wait_recv()
-        ccopy(12 + j, j, 1, 0, sib).start()
     local[3].wait()
     local[4].wait()
     pmat_all(0, 0, a0, p0)
+    for dz, dh in away:
+        ccopy((4 - dz) % 4 * 2 + dh, dz, dh, 0, q).wait_recv()
+        ccopy(8 + dz * 2 + dh, dz, dh, 0, sib).start()
     x_item(0)
     for i in range(2):
         take(OWN_SIB[i], kof(0, 0, 1), q, part(i))
-    for j in range(4):
-        ccopy(8 + j, j, 0, 1, q).wait_recv()
-        ccopy(12 + j, j, 1, 1, q).wait_recv()
+    ccopy(8, 0, 0, 1, q).wait_recv()
     pmat_all(0, 1, a1, p1)
+    for dz, dh in away:
+        ccopy(8 + dz * 2 + dh, dz, dh, 1, q).wait_recv()
     gmat_all(0, 0, p0)
     x_item(1)
     gmat_all(0, 1, p1)
@@ -295,12 +288,14 @@
         return remote(ysout.at[m], ysin.at[m], ssend.at[m], srecv.at[m], sib, t)
 
     def to_sibling(j, carry):
-        m = (chip + j) % 8
-        ysout[m] = ymat(m * 2 + 1 - c).astype(bf16)
-        scopy(m).start()
+        pair = [(chip + 2 * j + i) % 8 for i in range(2)]
+        for m, part_sum in [(m, ymat(m * 2 + 1 - c)) for m in pair]:
+            ysout[m] = part_sum.astype(bf16)
+        for m in pair:
+            scopy(m).start()
         return carry
 
-    lax.fori_loop(1, 9, to_sibling, 0)
+    lax.fori_loop(0, 4, to_sibling, 0)
 
     def ycopy(j, m, owner, peer):
         return remote(yout.at[m, peer], yin.at[chip, owner], ysend.at[j], yrecv.at[j], m * 2 + c, peer)
@@ -308,18 +303,24 @@
     own = pltpu.make_async_copy(yout.at[chip, t], yin.at[chip, t], yrecv.at[0])
 
     def to_owners(j, carry):
-        m = (chip + j) % 8
-        part_sum = ymat(m * 2 + c)
+        pair = [(chip + 2 * j + i) % 8 for i in (1, 2)]
+        sums = [ymat(m * 2 + c) for m in pair]
+        for m in pair:
+            scopy(m).wait_recv()
+        for m, part_sum in zip(pair, sums):
+            yout[m] = (part_sum + ysin[m].astype(f32)).astype(bf16)
+        for off, m in enumerate(pair):
+            for i in range(8):
+                ycopy(2 * j + 1 + off, m, t, (t + i) % 8).start()
+        return carry
+
+    lax.fori_loop(0, 3, to_owners, 0)
+    sums = [ymat((chip + 7) % 8 * 2 + c), ymat(q)]
+    for m, part_sum in zip(((chip + 7) % 8, chip), sums):
         scopy(m).wait_recv()
         yout[m] = (part_sum + ysin[m].astype(f32)).astype(bf16)
-        for i in range(8):
-            ycopy(j, m, t, (t + i) % 8).start()
-        return carry
-
-    lax.fori_loop(1, 8, to_owners, 0)
-    part_sum = ymat(q)
-    scopy(chip).wait_recv()
-    yout[chip] = (part_sum + ysin[chip].astype(f32)).astype(bf16)
+    for i in range(8):
+        ycopy(7, (chip + 7) % 8, t, (t + i) % 8).start()
     for i in range(1, 8):
         ycopy(0, chip, t, (t + i) % 8).start()
     own.start()

time: 68.9 us -> 66.3 us (0.962)
  Pallas kernels: 67.5 us -> 64.9 us
    pallas_call x1, Pallas kernels: 67.5 us -> 64.9 us  [shards(): pl.pallas_call(kernel, out_shape=jax.ShapeDtypeStruct(trials.shape, bf16)...]
where the time goes in v2:
time: 66.3 us; the launch traced here: 66.2 us
  Pallas kernels  64.9 us (98%)
  local copies, waits for them, and re-layouts  1.28 us (2%)
    pallas_call x1, Pallas kernels, shards(): pl.pallas_call(kernel, out_shape=jax.ShapeDtypeStruct(trials.shape, bf16)...  64.9 us

profile of v2, /device:TPU:1, one launch (start us, length us, event | category | flops | bytes accessed | tf_op | source)
XLA Modules:
  0.0 66.2 jit_solution(3323513010193656054)
XLA Ops:
  0.0 64.9 %shard_map.55 = bf16[1,4,512]{2,1,0:T(4,128)(2,1)} custom-call(bf16[1,4,512]{2,1,0:T(4,128)(2,1)} %x_hbm.1, bf16[1,256,2048]{2,1,0:T(8,128)(2,1)} %w_hbm.1, bf16[1,64,256]{2,1,0:T(8,128)(2,1)} %bitcast.2, bf16[1,64,256]{2,1,0:T(8,128)(2,1)} %bitcast.3, s32[16,16]{1,0:T(8,128)} %tab_hbm.1), custom_call_target="tpu_custom_call" | custom-call | tf_op jit(solution)/shard_map/pallas_call | solution.py:358
  64.9 1.3 %copy.7 = bf16[1,4,512]{2,1,0:T(4,128)(2,1)} copy(bf16[1,4,512]{2,1,0:T(4,128)(2,1)} %shard_map.55) | data formatting | bytes 8192

commit v3 on v2

--- a/solution.py
+++ b/solution.py
@@ -8,6 +8,8 @@
 MESH = pl.DeviceIdType.MESH
 bf16 = jnp.bfloat16
 f32 = jnp.float32
+f8 = jnp.float8_e4m3fn
+TINY = 2.0**-100
 NN = (((1,), (0,)), ((), ()))
 NT = (((1,), (1,)), ((), ()))
 TN = (((0,), (0,)), ((), ()))
@@ -27,7 +29,7 @@
 
 def kernel(
     x_hbm, w_hbm, uc_hbm, uv_hbm, tab_hbm, out_ref,
-    x_ref, w_ref, tab_ref, uv, xb, uc, p0, p1, a0, a1, g, ysout, ysin, yout, yin, xs, os,
+    x_ref, w_ref, tab_ref, uv, xb, uc, p0, p1, a0, a1, e0, e1, g, ysout, ysin, yout, yin, xs, os,
     lsem, tsend, trecv, ucsend, ucrecv, isend, irecv, ssend, srecv, ysend, yrecv,
 ):
     q = lax.axis_index("pb")
@@ -138,37 +140,31 @@
         for i in range(2):
             take(XC_SIB[i], kof(0, 1, 1), q, part(i))
 
-    def boundary_5():
-        take(DN_SIB[0], kof(3, 0, 1), q)
-
-    def boundary_6():
-        pass_on(1, XC_UP, XC_DN)
-
     def far(dh):
         k = kof(2, dh, 0)
         take(FAR_UP[dh], k, q, 0)
         take(FAR_DN[dh], k, q, 1)
         send(FAR_SIB[dh], k, sib)
 
-    def boundary_7():
+    def boundary_4():
+        take(DN_SIB[0], kof(3, 0, 1), q)
+
+    def boundary_6():
+        pass_on(1, XC_UP, XC_DN)
         take(UP_SIB[0], kof(1, 0, 1), q)
 
     def boundary_8():
         far(0)
-
-    def boundary_9():
         take(DN_SIB[1], kof(3, 1, 1), q)
 
     def boundary_10():
         far(1)
-
-    def boundary_11():
         take(UP_SIB[1], kof(1, 1, 1), q)
 
-    def boundary_13():
+    def boundary_12():
         take(FAR_SIB[0], kof(2, 0, 1), q)
 
-    def boundary_15():
+    def boundary_14():
         take(FAR_SIB[1], kof(2, 1, 1), q)
 
     def item(b2, dc):
@@ -176,20 +172,48 @@
         dh = jnp.where(b2 < 2, b2, jnp.where(b2 < 4, 0, jnp.where(b2 < 6, 1, b2 - 6)))
         return kof(dz, dh, dc)
 
-    def amat(k, a):
-        u = uc[k // 4, k % 4]
+    lane = lax.broadcasted_iota(jnp.int32, (64, 128), 1)
+    column = lax.broadcasted_iota(jnp.int32, (256, 128), 1)
+
+    def level(top):
+        return jnp.floor(jnp.log2(jnp.maximum(top, TINY)))
+
+    def split(value):
+        hi = value.astype(f8)
+        return hi, (value - hi.astype(f32)).astype(f8)
+
+    def amat(k, a, back):
+        u = jnp.transpose(uc[k // 4, k % 4].astype(f32)).astype(bf16)
         xk = xb[k].astype(f32)
+        tops = jnp.zeros((256, 128), f32)
+        values = []
         for sh in range(2):
-            xm = xk[:, sh * 8 : sh * 8 + 8, :].reshape(64, 128).astype(bf16)
-            both = dot(u, xm, TN).astype(bf16)
-            a[2 * sh] = both[:, :64]
-            a[2 * sh + 1] = both[:, 64:]
+            xm = xk[:, sh * 8 : sh * 8 + 8, :].reshape(64, 128)
+            xr = pltpu.roll(xm, 64, 1)
+            twice = [jnp.where((lane < 64) == (sl == 0), xm, xr).astype(bf16) for sl in range(2)]
+            both = dot(u, jnp.concatenate(twice, axis=1), NN).astype(bf16).astype(f32)
+            for sl in range(2):
+                av = both[:, sl * 128 : sl * 128 + 128]
+                top = jnp.max(jnp.abs(av), axis=1, keepdims=True)
+                tops = jnp.where(column == 2 * sh + sl, top, tops)
+                values.append(av)
+        levels = level(tops)
+        scale = jnp.exp2(7.0 - levels)
+        for s, av in enumerate(values):
+            hi, lo = split(av * scale[:, s : s + 1])
+            a[s, :, :128] = hi
+            a[s, :, 128:] = lo
+        back[...] = jnp.exp2(jnp.transpose(levels)[:8] - 7.0)
 
     def pmat(k, a, p, b):
         n = slice(b * 256, b * 256 + 256)
-        wb = w_ref[:, n].astype(f32)
+        ub = uv[k, b].astype(f32)
+        lev = level(jnp.max(jnp.abs(ub), axis=0, keepdims=True))
+        hi, lo = split(ub * jnp.exp2(7.0 - lev))
+        u8 = jnp.concatenate([hi, lo, hi, lo], axis=0)
+        wb = w_ref[:, n].astype(f32) * jnp.exp2(lev - 7.0)
         for s in range(4):
-            p[s, :, n] = (dot(a[s], uv[k, b], NN) * wb).astype(bf16)
+            p[s, :, n] = (dot(a[s], u8, NN) * wb).astype(bf16)
 
     def partner(kp):
         k = jnp.int32(0)
@@ -197,30 +221,33 @@
             k = jnp.where(tab_ref[i, q] == kp, i, k)
         return k
 
-    def gmat(u, kp, p, b):
+    def scaled(kp, back):
+        kk = partner(kp)
+        u = uc[kk // 4, kk % 4].astype(f32)
+        return [(u * back[s : s + 1, :]).astype(bf16) for s in range(4)]
+
+    def gmat(us, kp, p, b):
         n = slice(b * 256, b * 256 + 256)
         for s in range(4):
-            g[kp, s * 64 : s * 64 + 64, n] = dot(u, p[s, :, n], NN).astype(bf16)
-
-    def half(b2, dc, b2n, dcn, pr, pw, an):
-        kp, kn = item(b2, dc), item(b2n, dcn)
-        kk = partner(kp)
-        u = uc[kk // 4, kk % 4]
-        amat(kn, an)
-        for b in range(8):
-            gmat(u, kp, pr, b)
-            pmat(kn, an, pw, b)
-
-    def gmat_all(b2, dc, p):
+            g[kp, s * 64 : s * 64 + 64, n] = dot(us[s], p[s, :, n], NN).astype(bf16)
+
+    def half(g_item, m_item, a_item, pr, pw, am, aw, back):
+        us = scaled(g_item, back)
+        for b in range(8):
+            gmat(us, g_item, pr, b)
+            pmat(m_item, am, pw, b)
+            if b == 3 and a_item is not None:
+                amat(a_item, aw, back)
+
+    def gmat_all(b2, dc, p, back):
         kp = item(b2, dc)
-        kk = partner(kp)
-        u = uc[kk // 4, kk % 4]
-        for b in range(8):
-            gmat(u, kp, p, b)
-
-    def pmat_all(b2, dc, a, p):
+        us = scaled(kp, back)
+        for b in range(8):
+            gmat(us, kp, p, b)
+
+    def pmat_all(b2, dc, a, p, back):
         k = item(b2, dc)
-        amat(k, a)
+        amat(k, a, back)
         for b in range(8):
             pmat(k, a, p, b)
 
@@ -240,39 +267,37 @@
     send_own(1)
     local[3].wait()
     local[4].wait()
-    pmat_all(0, 0, a0, p0)
+    pmat_all(0, 0, a0, p0, e0)
     for dz, dh in away:
         ccopy((4 - dz) % 4 * 2 + dh, dz, dh, 0, q).wait_recv()
         ccopy(8 + dz * 2 + dh, dz, dh, 0, sib).start()
-    x_item(0)
     for i in range(2):
         take(OWN_SIB[i], kof(0, 0, 1), q, part(i))
     ccopy(8, 0, 0, 1, q).wait_recv()
-    pmat_all(0, 1, a1, p1)
+    pmat_all(0, 1, a1, p1, e1)
+    x_item(0)
     for dz, dh in away:
         ccopy(8 + dz * 2 + dh, dz, dh, 1, q).wait_recv()
-    gmat_all(0, 0, p0)
+    gmat_all(0, 0, p0, e0)
     x_item(1)
-    gmat_all(0, 1, p1)
+    gmat_all(0, 1, p1, e1)
+    pmat_all(1, 0, a0, p0, e0)
     pass_on(0, OWN_UP, OWN_DN)
-    pmat_all(1, 0, a0, p0)
-
-    odd = {3: boundary_3, 5: boundary_5, 7: boundary_7, 9: boundary_9, 11: boundary_11, 13: boundary_13}
-    even = {6: boundary_6, 8: boundary_8, 10: boundary_10}
+
+    boundary_3()
+    amat(item(1, 1), a1, e1)
+    acts = {4: boundary_4, 6: boundary_6, 8: boundary_8, 10: boundary_10, 12: boundary_12, 14: boundary_14}
 
     def body(j, carry):
-        for b, act in odd.items():
-            pl.when(2 * j + 3 == b)(act)
-        half(j + 1, 0, j + 1, 1, p0, p1, a1)
-        for b, act in even.items():
+        half(item(j + 1, 0), item(j + 1, 1), item(j + 2, 0), p0, p1, a1, a0, e0)
+        for b, act in acts.items():
             pl.when(2 * j + 4 == b)(act)
-        half(j + 1, 1, j + 2, 0, p1, p0, a0)
+        half(item(j + 1, 1), item(j + 2, 0), item(j + 2, 1), p1, p0, a0, a1, e1)
         return carry
 
     lax.fori_loop(0, 6, body, 0)
-    boundary_15()
-    half(7, 0, 7, 1, p0, p1, a1)
-    gmat_all(7, 1, p1)
+    half(item(7, 0), item(7, 1), None, p0, p1, a1, a0, e0)
+    gmat_all(7, 1, p1, e1)
 
     def ymat(k):
         kp = tab_ref[k, q]
@@ -369,8 +394,10 @@
             pltpu.VMEM((4, 4, 64, 256), bf16),
             pltpu.VMEM((4, 256, 2048), bf16),
             pltpu.VMEM((4, 256, 2048), bf16),
-            pltpu.VMEM((4, 256, 64), bf16),
-            pltpu.VMEM((4, 256, 64), bf16),
+            pltpu.VMEM((4, 256, 256), f8),
+            pltpu.VMEM((4, 256, 256), f8),
+            pltpu.VMEM((8, 256), f32),
+            pltpu.VMEM((8, 256), f32),
             pltpu.VMEM((16, 256, 2048), bf16),
             pltpu.VMEM((8, 8, 16, 128), bf16),
             pltpu.VMEM((8, 8, 16, 128), bf16),

time: 66.3 us -> 63.7 us (0.961)
  Pallas kernels: 64.9 us -> 62.3 us
    pallas_call x1, Pallas kernels: 64.9 us -> 62.3 us  [shards(): pl.pallas_call(kernel, out_shape=jax.ShapeDtypeStruct(trials.shape, bf16)...]
where the time goes in v3:
time: 63.7 us; the launch traced here: 63.6 us
  Pallas kernels  62.3 us (98%)
  local copies, waits for them, and re-layouts  1.28 us (2%)
    pallas_call x1, Pallas kernels, shards(): pl.pallas_call(kernel, out_shape=jax.ShapeDtypeStruct(trials.shape, bf16)...  62.3 us
    unnamed x1, local copies, waits for them, and re-layouts  1.28 us

profile of v3, /device:TPU:1, one launch (start us, length us, event | category | flops | bytes accessed | tf_op | source)
XLA Modules:
  0.0 63.6 jit_solution(11476821017635818500)
XLA Ops:
  0.0 62.3 %shard_map.55 = bf16[1,4,512]{2,1,0:T(4,128)(2,1)} custom-call(bf16[1,4,512]{2,1,0:T(4,128)(2,1)} %x_hbm.1, bf16[1,256,2048]{2,1,0:T(8,128)(2,1)} %w_hbm.1, bf16[1,64,256]{2,1,0:T(8,128)(2,1)} %bitcast.2, bf16[1,64,256]{2,1,0:T(8,128)(2,1)} %bitcast.3, s32[16,16]{1,0:T(8,128)} %tab_hbm.1), custom_call_target="tpu_custom_call" | custom-call | tf_op jit(solution)/shard_map/pallas_call | solution.py:383
  62.3 1.3 %copy.7 = bf16[1,4,512]{2,1,0:T(4,128)(2,1)} copy(bf16[1,4,512]{2,1,0:T(4,128)(2,1)} %shard_map.55) | data formatting | bytes 8192

commit v4 on v3

--- a/solution.py
+++ b/solution.py
@@ -182,28 +182,26 @@
         hi = value.astype(f8)
         return hi, (value - hi.astype(f32)).astype(f8)
 
-    def amat(k, a, back):
+    def amat_parts(k, a, back):
         u = jnp.transpose(uc[k // 4, k % 4].astype(f32)).astype(bf16)
         xk = xb[k].astype(f32)
-        tops = jnp.zeros((256, 128), f32)
-        values = []
-        for sh in range(2):
-            xm = xk[:, sh * 8 : sh * 8 + 8, :].reshape(64, 128)
-            xr = pltpu.roll(xm, 64, 1)
-            twice = [jnp.where((lane < 64) == (sl == 0), xm, xr).astype(bf16) for sl in range(2)]
-            both = dot(u, jnp.concatenate(twice, axis=1), NN).astype(bf16).astype(f32)
-            for sl in range(2):
-                av = both[:, sl * 128 : sl * 128 + 128]
-                top = jnp.max(jnp.abs(av), axis=1, keepdims=True)
-                tops = jnp.where(column == 2 * sh + sl, top, tops)
-                values.append(av)
-        levels = level(tops)
-        scale = jnp.exp2(7.0 - levels)
-        for s, av in enumerate(values):
-            hi, lo = split(av * scale[:, s : s + 1])
+        levels = jnp.zeros((256, 128), f32)
+        for s in range(4):
+            xm = xk[:, s // 2 * 8 : s // 2 * 8 + 8, :].reshape(64, 128)
+            twice = jnp.where((lane < 64) == (s % 2 == 0), xm, pltpu.roll(xm, 64, 1)).astype(bf16)
+            av = dot(u, twice, NN).astype(bf16).astype(f32)
+            lev = level(jnp.max(jnp.abs(av), axis=1, keepdims=True))
+            levels = jnp.where(column == s, lev, levels)
+            hi, lo = split(av * jnp.exp2(7.0 - lev))
             a[s, :, :128] = hi
             a[s, :, 128:] = lo
-        back[...] = jnp.exp2(jnp.transpose(levels)[:8] - 7.0)
+            if s == 3:
+                back[...] = jnp.exp2(jnp.transpose(levels)[:8] - 7.0)
+            yield
+
+    def amat(k, a, back):
+        for _ in amat_parts(k, a, back):
+            pass
 
     def pmat(k, a, p, b):
         n = slice(b * 256, b * 256 + 256)
@@ -233,11 +231,12 @@
 
     def half(g_item, m_item, a_item, pr, pw, am, aw, back):
         us = scaled(g_item, back)
+        parts = iter(()) if a_item is None else amat_parts(a_item, aw, back)
         for b in range(8):
             gmat(us, g_item, pr, b)
             pmat(m_item, am, pw, b)
-            if b == 3 and a_item is not None:
-                amat(a_item, aw, back)
+            if b % 2 == 0:
+                next(parts, None)
 
     def gmat_all(b2, dc, p, back):
         kp = item(b2, dc)

time: 63.7 us -> 63.6 us (level)
  no operation moved by 1% of the time
where the time goes in v4:
time: 63.6 us; the launch traced here: 63.4 us
  Pallas kernels  62.1 us (98%)
  local copies, waits for them, and re-layouts  1.28 us (2%)
    pallas_call x1, Pallas kernels, shards(): pl.pallas_call(kernel, out_shape=jax.ShapeDtypeStruct(trials.shape, bf16)...  62.1 us
    unnamed x1, local copies, waits for them, and re-layouts  1.28 us

profile of v4, /device:TPU:1, one launch (start us, length us, event | category | flops | bytes accessed | tf_op | source)
XLA Modules:
  0.0 63.4 jit_solution(15895902879162315341)
XLA Ops:
  0.0 62.1 %shard_map.55 = bf16[1,4,512]{2,1,0:T(4,128)(2,1)} custom-call(bf16[1,4,512]{2,1,0:T(4,128)(2,1)} %x_hbm.1, bf16[1,256,2048]{2,1,0:T(8,128)(2,1)} %w_hbm.1, bf16[1,64,256]{2,1,0:T(8,128)(2,1)} %bitcast.2, bf16[1,64,256]{2,1,0:T(8,128)(2,1)} %bitcast.3, s32[16,16]{1,0:T(8,128)} %tab_hbm.1), custom_call_target="tpu_custom_call" | custom-call | tf_op jit(solution)/shard_map/pallas_call | solution.py:382
  62.1 1.3 %copy.7 = bf16[1,4,512]{2,1,0:T(4,128)(2,1)} copy(bf16[1,4,512]{2,1,0:T(4,128)(2,1)} %shard_map.55) | data formatting | bytes 8192
